TPU v7x, 128 devices: a whole 4x4x4 slice. The times are simulated.
128 devices in a mesh: dp: 16 (over y, x), expert: 8 (over z, core).
Axes of the slice: x: 4, y: 4, z: 4, core: 2. Of those that a mesh axis runs over, the one named last changes fastest.
Arguments:
- tokens: bfloat16 [16384, 1280], P(('dp', 'expert')), may hold values from -6 to 6
- cotangent: bfloat16 [16384, 1280], P(('dp', 'expert')), may hold values from -4 to 4
- gate_weights: float32 [16384, 2], P(('dp', 'expert')), may hold values from 0.1 to 1
- expert_ids: int32 [16384, 2], P(('dp', 'expert')), may hold values from 0 to 15, as said below
- segments: int32 [128, 128], P(('dp', 'expert')), may hold values from 0 to 3, never falling along the last dimension, each value on 1 to 64 neighbouring positions
- keep_counts: int32 [128, 4], P(('dp', 'expert')), may hold values from 1 to 64
- expand_weight: bfloat16 [16, 2560, 1280], P('expert', 'dp'), may hold values from -0.15625 to 0.15625
- reduce_weight: bfloat16 [16, 2560, 1280], P('expert', 'dp'), may hold values from -0.125 to 0.125
Outputs:
- output: bfloat16 [16384, 1280], P(('dp', 'expert'))
- tokens_grad: bfloat16 [16384, 1280], P(('dp', 'expert'))
- gating_grad: float32 [16384, 2], P(('dp', 'expert'))
- expand_grad: bfloat16 [16, 2560, 1280], P('expert', 'dp')
- reduce_grad: bfloat16 [16, 2560, 1280], P('expert', 'dp')
Inputs may be any that keep to these rules, and one draw needn't show every extreme that they name: `expert_ids`: the 128 tokens of one sequence name each expert exactly 16 times, and a token's 2 experts differ. `segments`: within a sequence the ids never fall, every image 0 to 3 appears, each holds 1 to 64 positions.
All inputs are finite; a program needn't handle non-finite values.
Results may differ from a plain program's by a relative error of at most 0.015.
Values may be sent and summed in bfloat16 or wider, within the bound.
A program may use at most 128 MiB of HBM per device.

v0:
```python
import jax
import jax.numpy as jnp
from jax import lax
from jax.sharding import PartitionSpec as P

epsilon = 1e-06
root_half = 0.7071067811865476
density_scale = 0.3989422804014327


def gelu_value(values):
    return 0.5 * values * (1.0 + jax.scipy.special.erf(values * root_half))


def gelu_slope(values):
    return (
        0.5 * (1.0 + jax.scipy.special.erf(values * root_half))
        + values * jnp.exp(-0.5 * values * values) * density_scale
    )


def project_up(rows, weight):
    return jnp.einsum("rld,lhd->rlh", rows, weight, preferred_element_type=jnp.float32)


def project_down(hidden, weight):
    return jnp.einsum("rlh,lhd->rld", hidden, weight, preferred_element_type=jnp.float32)


def outer_rows(left, right):
    return jnp.einsum("rlh,rld->lhd", left, right, preferred_element_type=jnp.float32)


def body(
    tokens, cotangent, gate_weights, expert_ids, segments, keep_counts, expand_weight, reduce_weight
):
    tok_count = tokens.shape[0]
    top_count = expert_ids.shape[1]
    width = tokens.shape[1]
    sources = lax.axis_size("expert")
    local = expand_weight.shape[0]
    total_experts = local * sources
    pick_count = top_count * tok_count
    capacity = pick_count // total_experts
    image_ids = segments[0]
    position = jnp.arange(tok_count, dtype=jnp.int32)
    earlier_img = jnp.sum((image_ids[None, :] < image_ids[:, None]).astype(jnp.int32), axis=1)
    image_match = (
        image_ids[:, None] == jnp.arange(keep_counts.shape[1], dtype=jnp.int32)[None, :]
    ).astype(jnp.int32)
    keep_token = jnp.sum(image_match * keep_counts, axis=1)
    alive = (position - earlier_img < keep_token).astype(jnp.float32)
    tokens_wide = tokens.astype(jnp.float32)
    mean_rows = jnp.mean(tokens_wide, axis=1, keepdims=True)
    centred = tokens_wide - mean_rows
    inv_scale = lax.rsqrt(jnp.mean(centred * centred, axis=1, keepdims=True) + epsilon)
    normed = centred * inv_scale
    normed_low = normed.astype(jnp.bfloat16)
    choice_list = expert_ids.reshape(-1)
    matches = (choice_list[:, None] == jnp.arange(total_experts, dtype=jnp.int32)[None, :]).astype(
        jnp.int32
    )
    before = jnp.cumsum(matches, axis=0) - matches
    slot_list = jnp.sum(before * matches, axis=1)
    target = choice_list * capacity + slot_list
    order = (
        jnp.zeros((pick_count,), jnp.int32).at[target].set(jnp.arange(pick_count, dtype=jnp.int32))
    )
    source = order // top_count
    alive_pick = jnp.repeat(alive, top_count)
    weight_pick = gate_weights.reshape(-1) * alive_pick
    sent_rows = jnp.where(
        alive_pick[order][:, None] > 0, normed_low[source], jnp.zeros((), jnp.bfloat16)
    )
    cot_wide = cotangent.astype(jnp.float32)
    sent_grads = (cot_wide[source] * weight_pick[order][:, None]).astype(jnp.bfloat16)

    def to_slots(flat):
        return (
            flat.reshape(sources, local, capacity, width)
            .transpose(0, 2, 1, 3)
            .reshape(sources * capacity, local, width)
        )

    def from_slots(rows):
        return (
            rows.reshape(sources, capacity, local, width)
            .transpose(0, 2, 1, 3)
            .reshape(pick_count, width)
        )

    arrived = to_slots(lax.all_to_all(sent_rows, "expert", split_axis=0, concat_axis=0, tiled=True))
    arrived_grads = to_slots(
        lax.all_to_all(sent_grads, "expert", split_axis=0, concat_axis=0, tiled=True)
    )
    slot_rows = arrived.shape[0]
    all_rows = lax.all_gather(arrived, "dp", axis=0, tiled=True)
    pre = project_up(all_rows, expand_weight)
    hidden = gelu_value(pre).astype(jnp.bfloat16)
    results = lax.psum_scatter(
        project_down(hidden, reduce_weight).astype(jnp.bfloat16),
        "dp",
        scatter_dimension=0,
        tiled=True,
    )
    all_grads = lax.all_gather(arrived_grads, "dp", axis=0, tiled=True)
    back_hidden = project_up(all_grads, reduce_weight)
    dpre = (back_hidden * gelu_slope(pre)).astype(jnp.bfloat16)
    input_rows = lax.psum_scatter(
        project_down(dpre, expand_weight).astype(jnp.bfloat16),
        "dp",
        scatter_dimension=0,
        tiled=True,
    )

    def add_block(block, totals):
        offset = block * slot_rows
        hidden_block = lax.dynamic_slice_in_dim(hidden, offset, slot_rows, 0)
        dpre_block = lax.dynamic_slice_in_dim(dpre, offset, slot_rows, 0)
        grad_block = lax.dynamic_slice_in_dim(all_grads, offset, slot_rows, 0)
        row_block = lax.dynamic_slice_in_dim(all_rows, offset, slot_rows, 0)
        second_piece = lax.optimization_barrier(
            outer_rows(hidden_block, grad_block).astype(jnp.bfloat16)
        ).astype(jnp.float32)
        first_piece = lax.optimization_barrier(
            outer_rows(dpre_block, row_block).astype(jnp.bfloat16)
        ).astype(jnp.float32)
        return (totals[0] + first_piece, totals[1] + second_piece)

    empty = jnp.zeros(expand_weight.shape, jnp.float32)
    first_total, second_total = lax.fori_loop(
        0, all_rows.shape[0] // slot_rows, add_block, (empty, empty)
    )
    expand_grad = first_total.astype(jnp.bfloat16)
    reduce_grad = second_total.astype(jnp.bfloat16)
    returned = lax.all_to_all(
        from_slots(results), "expert", split_axis=0, concat_axis=0, tiled=True
    )
    result_pick = returned[target].astype(jnp.float32).reshape(tok_count, top_count, -1)
    output = (
        tokens_wide + jnp.sum(result_pick * weight_pick.reshape(tok_count, top_count, 1), axis=1)
    ).astype(jnp.bfloat16)
    gating_grad = alive_pick.reshape(tok_count, top_count) * jnp.sum(
        cot_wide[:, None, :] * result_pick, axis=2
    )
    returned_grads = lax.all_to_all(
        from_slots(input_rows), "expert", split_axis=0, concat_axis=0, tiled=True
    )
    input_pick = returned_grads[target].astype(jnp.float32).reshape(tok_count, top_count, -1)
    grad_norm = jnp.sum(input_pick * alive_pick.reshape(tok_count, top_count, 1), axis=1)
    tokens_grad = cot_wide + inv_scale * (
        grad_norm
        - jnp.mean(grad_norm, axis=1, keepdims=True)
        - normed * jnp.mean(grad_norm * normed, axis=1, keepdims=True)
    )
    return (output, tokens_grad.astype(jnp.bfloat16), gating_grad, expand_grad, reduce_grad)


def solution(mesh):
    in_specs = (
        P(("dp", "expert"), None),
        P(("dp", "expert"), None),
        P(("dp", "expert"), None),
        P(("dp", "expert"), None),
        P(("dp", "expert"), None),
        P(("dp", "expert"), None),
        P("expert", "dp", None),
        P("expert", "dp", None),
    )
    out_specs = (
        P(("dp", "expert"), None),
        P(("dp", "expert"), None),
        P(("dp", "expert"), None),
        P("expert", "dp", None),
        P("expert", "dp", None),
    )
    return jax.shard_map(body, mesh=mesh, in_specs=in_specs, out_specs=out_specs, check_vma=False)
```

profile of v0, /device:TPU:1, one launch (start us, length us, event | category | flops | bytes accessed | tf_op | source)
XLA Modules:
  0.0 434.9 jit_solution(15564184737724795476)
XLA Ops:
  16.0 1.9 gather_fusion
  19.6 17.6 %all_to_all.36 = bf16[8,32,1280]{2,1,0:T(8,128)(2,1)S(1)} all-to-all(bf16[8,32,1280]{2,1,0:T(8,128)(2,1)S(1)} %broadcast_select_fusion), channel_id=1, replica_groups=mesh['dp'=16,'expert'=8] {'expert'}, dimensions={0} | all-to-all | bytes 1310720 | tf_op jit(solution)/shard_map/all_to_all | solution.py:92
  38.4 1.9 gather_fusion.4
  41.9 14.2 %all_to_all.37 = bf16[8,32,1280]{2,1,0:T(8,128)(2,1)S(1)} all-to-all(bf16[8,32,1280]{2,1,0:T(8,128)(2,1)S(1)} %multiply_convert_fusion.1), channel_id=1, replica_groups=mesh['dp'=16,'expert'=8] {'expert'}, dimensions={0} | all-to-all | bytes 1310720 | tf_op jit(solution)/shard_map/all_to_all | solution.py:94
  57.1 61.1 %all-gather.3.cloned.1.call-done = bf16[2048,2,1280]{2,0,1:T(8,128)(2,1)} async-done(((bf16[128,2,1280]{2,0,1:T(8,128)(2,1)}), bf16[2048,2,1280]{2,0,1:T(8,128)(2,1)}) %all-gather.3.cloned.1.call-update) | async-done | bytes 10485776 | tf_op jit(solution)/shard_map/all_gather | solution.py:97
  118.2 9.1 %multiply_convert_fusion = (bf16[2048,2,160]{0,2,1:T(8,128)(2,1)S(1)}, f32[2048,2,160]{0,2,1:T(8,128)}) fusion(bf16[2048,2,1280]{2,0,1:T(8,128)(2,1)} %all-gather.3.cloned.1.call-done, bf16[2,160,1280]{2,1,0:T(8,128)(2,1)S(1)} %copy-done), kind=kOutput, calls=%fused_computation.30 | convolution fusion | flops 1680998400 | bytes 15237120 | tf_op jit(solution)/shard_map/rld,lhd->rlh/dot_general | solution.py:23
  127.3 73.6 %all-gather.5.cloned.1.call-done = bf16[2048,2,1280]{2,0,1:T(8,128)(2,1)} async-done(((bf16[128,2,1280]{2,0,1:T(8,128)(2,1)}), bf16[2048,2,1280]{2,0,1:T(8,128)(2,1)}) %all-gather.5.cloned.1.call-update) | async-done | bytes 10485776 | tf_op jit(solution)/shard_map/all_gather | solution.py:106
  200.9 8.6 %fusion.9 = bf16[2048,2,160]{0,2,1:T(8,128)(2,1)S(1)} fusion(bf16[2048,2,1280]{2,0,1:T(8,128)(2,1)} %all-gather.5.cloned.1.call-done, bf16[2,160,1280]{2,1,0:T(8,128)(2,1)} %param.17, f32[2048,2,160]{0,2,1:T(8,128)} %get-tuple-element.189), kind=kOutput, calls=%fused_computation.25 | convolution fusion | flops 1684275200 | bytes 15237120 | tf_op jit(solution)/shard_map/rld,lhd->rlh/dot_general | solution.py:23
  210.6 5.6 %fusion.7 = bf16[2048,2,1280]{2,0,1:T(8,128)(2,1)} fusion(bf16[2048,2,160]{0,2,1:T(8,128)(2,1)S(1)} %fusion.9, bf16[2,160,1280]{2,1,0:T(8,128)(2,1)S(1)} %copy-done), kind=kOutput, calls=%fused_computation.20 | convolution fusion | flops 1682964480 | bytes 12615680 | tf_op jit(solution)/shard_map/rlh,lhd->rld/dot_general | solution.py:27
  217.3 5.7 %fusion.6 = bf16[2048,2,1280]{2,0,1:T(8,128)(2,1)} fusion(bf16[2048,2,160]{0,2,1:T(8,128)(2,1)S(1)} %get-tuple-element.244, bf16[2,160,1280]{2,1,0:T(8,128)(2,1)S(1)} %copy-done.10), kind=kOutput, calls=%fused_computation.19 | convolution fusion | flops 1682964480 | bytes 12615680 | tf_op jit(solution)/shard_map/rlh,lhd->rld/dot_general | solution.py:27
  223.1 81.8 %reduce-scatter.5.cloned.1.call-done = bf16[128,2,1280]{2,0,1:T(8,128)(2,1)} async-done(((bf16[2048,2,1280]{2,0,1:T(8,128)(2,1)}), bf16[128,2,1280]{2,0,1:T(8,128)(2,1)}) %reduce-scatter.5.cloned.1.call-update) | async-done | bytes 655376 | tf_op jit(solution)/shard_map/reduce_scatter | solution.py:109
  304.9 2.0 copy.47
  306.9 5.9 %all-to-all-start.3 = ((bf16[8,32,1280]{2,1,0:T(8,128)(2,1)}), bf16[8,32,1280]{2,1,0:T(8,128)(2,1)}, u32[]{:S(2)}, u32[]{:S(2)}) async-start(bf16[8,32,1280]{2,1,0:T(8,128)(2,1)} %bitcast.23), calls=%async_computation.5 | async-start | bytes 1310720 | tf_op jit(solution)/shard_map/all_to_all | solution.py:146
  312.8 86.8 %while.16 = (s32[]{:T(128)}, f32[2,160,1280]{2,1,0:T(8,128)}, f32[2,160,1280]{2,1,0:T(8,128)S(1)}, bf16[2048,2,160]{0,2,1:T(8,128)(2,1)}, bf16[2048,2,1280]{2,0,...) while((s32[]{:T(128)}, f32[2,160,1280]{2,1,0:T(8,128)}, ...), condition=%wide.region_17.18_spmd.clone, body=%wide.region_16.17_spmd.clone.sunk | while | flops 212992000 | bytes 24414436 | solution.py:131
  334.6 1.6 convolution_convert_fusion.6
  361.8 1.6 convolution_convert_fusion.6
  402.3 2.0 copy.42
  404.3 4.8 %all-to-all-start.1 = ((bf16[8,32,1280]{2,1,0:T(8,128)(2,1)}), bf16[8,32,1280]{2,1,0:T(8,128)(2,1)S(1)}, u32[]{:S(2)}, u32[]{:S(2)}) async-start(bf16[8,32,1280]{2,1,0:T(8,128)(2,1)} %bitcast.13), calls=%async_computation.2 | async-start | bytes 1310720 | tf_op jit(solution)/shard_map/all_to_all | solution.py:136
  409.1 2.9 gather_fusion.5
  412.4 1.7 reshape.174
  414.2 3.0 multiply_reduce_fusion.2
  417.6 2.5 all-to-all-done.1
  421.3 1.7 reshape.173
  423.0 3.5 multiply_reduce_fusion
  (197 shorter events, 106.0 us)
Async XLA Ops:
  7.2 111.0 %copy-start = (bf16[2,160,1280]{2,1,0:T(8,128)(2,1)S(1)}, bf16[2,160,1280]{2,1,0:T(8,128)(2,1)}, u32[]{:S(2)}) copy-start(bf16[2,160,1280]{2,1,0:T(8,128)(2,1)} %param.16) | copy-start | bytes 2457604
  7.2 10.8 %copy-start.5 = (bf16[128,1280]{1,0:T(8,128)(2,1)S(1)}, bf16[128,1280]{1,0:T(8,128)(2,1)}, u32[]{:S(2)}) copy-start(bf16[128,1280]{1,0:T(8,128)(2,1)} %param.10) | copy-start | bytes 983044
  7.2 111.0 %all-gather.3.cloned.1.call-start = ((), (), s32[]{:S(2)}) async-start(), calls=%async_computation.6 | async-start | bytes 11141120 | tf_op jit(solution)/shard_map/all_gather | solution.py:97
  19.6 18.5 %copy-start.11 = (f32[128,2]{0,1:T(2,128)S(1)}, f32[128,2]{0,1:T(2,128)}, u32[]{:S(2)}) copy-start(f32[128,2]{0,1:T(2,128)} %param.12) | copy-start | bytes 3076
  37.2 3.3 copy-start.8
  38.1 162.8 %all-gather.5.cloned.1.call-start = ((), (), s32[]{:S(2)}) async-start(), calls=%async_computation.8 | async-start | bytes 11141120 | tf_op jit(solution)/shard_map/all_gather | solution.py:106
  57.0 247.9 %reduce-scatter.5.cloned.1.call-start = ((), (), s32[]{:S(2)}) async-start(), calls=%async_computation.9 | async-start | bytes 11141120 | tf_op jit(solution)/shard_map/reduce_scatter | solution.py:109
  127.3 89.1 %copy-start.6 = (bf16[2048,2,160]{0,2,1:T(8,128)(2,1)}, bf16[2048,2,160]{0,2,1:T(8,128)(2,1)S(1)}, u32[]{:S(2)}) copy-start(bf16[2048,2,160]{0,2,1:T(8,128)(2,1)S(1)} %get-tuple-element.244) | copy-start | bytes 3932164
  216.2 186.2 %reduce-scatter.3.cloned.1.call-start = ((), (), s32[]{:S(2)}) async-start(), calls=%async_computation.7 | async-start | bytes 11141120 | tf_op jit(solution)/shard_map/reduce_scatter | solution.py:100
  306.9 97.5 %all-to-all-start.3 = ((bf16[8,32,1280]{2,1,0:T(8,128)(2,1)}), bf16[8,32,1280]{2,1,0:T(8,128)(2,1)}, u32[]{:S(2)}, u32[]{:S(2)}) async-start(bf16[8,32,1280]{2,1,0:T(8,128)(2,1)} %bitcast.23), calls=%async_computation.5 | async-start | bytes 1310720 | tf_op jit(solution)/shard_map/all_to_all | solution.py:146
  318.2 3.1 copy-start.2
  323.6 3.2 copy-start.2
  329.1 3.2 copy-start.2
  334.6 3.2 copy-start.2
  340.0 3.2 copy-start.2
  345.5 3.1 copy-start.2
  356.3 3.1 copy-start.2
  361.8 3.1 copy-start.2
  367.2 3.1 copy-start.2
  388.8 3.2 copy-start.2
  394.2 3.2 copy-start.2
  404.3 15.7 %all-to-all-start.1 = ((bf16[8,32,1280]{2,1,0:T(8,128)(2,1)}), bf16[8,32,1280]{2,1,0:T(8,128)(2,1)S(1)}, u32[]{:S(2)}, u32[]{:S(2)}) async-start(bf16[8,32,1280]{2,1,0:T(8,128)(2,1)} %bitcast.13), calls=%async_computation.2 | async-start | bytes 1310720 | tf_op jit(solution)/shard_map/all_to_all | solution.py:136
  423.0 4.2 copy-start.9
  423.0 5.4 %copy-start.1 = (bf16[2,160,1280]{2,1,0:T(8,128)(2,1)S(1)}, bf16[2,160,1280]{2,1,0:T(8,128)(2,1)}, u32[]{:S(2)}) copy-start(bf16[2,160,1280]{2,1,0:T(8,128)(2,1)} %param.16) | copy-start | bytes 2457604
  (24 other events, 38.6 us)
Sparse Core Ops, SparseCore 0:
  38.2 79.9 all-gather.2
  120.9 79.9 all-gather.4
  216.3 88.5 reduce-scatter.4
  308.2 88.6 reduce-scatter.2
where the time goes:
time: 436 us; the launch traced here: 435 us
  waiting for transfers between devices  219 us (50%)
  matrix products  79 us (18%)
  local copies, waits for them, and re-layouts  45.8 us (11%)
  other arithmetic  33.5 us (8%)
  blocking collectives  31.8 us (7%)
  between operations  14 us (3%)
  starting transfers between devices  11.1 us (3%)
    reduce_scatter x1, waiting for transfers between devices, body(): lax.psum_scatter(project_down(dpre, expand_weight).astype(jnp.bfloat16),...  81.8 us
    all_gather x1, waiting for transfers between devices, body(): all_grads = lax.all_gather(arrived_grads, 'dp', axis=0, tiled=True)  73.6 us
    all_gather x1, waiting for transfers between devices, body(): all_rows = lax.all_gather(arrived, 'dp', axis=0, tiled=True)  61.1 us
    dot_general x32, matrix products, outer_rows(): jnp.einsum('rlh,rld->lhd', left, right, preferred_element_type=jnp.float32)  50.1 us
    while x64, local copies, waits for them, and re-layouts  19 us
    dot_general x2, matrix products, project_up(): jnp.einsum('rld,lhd->rlh', rows, weight, preferred_element_type=jnp.float32)  17.7 us
    all_to_all x1, blocking collectives, body(): lax.all_to_all(sent_rows, 'expert', split_axis=0, concat_axis=0, tiled=True)  17.6 us
    add x16, other arithmetic, add_block(): return (totals[0] + first_piece, totals[1] + second_piece)  17.2 us
  transfers between devices with their start and end apart: 6, of which 4 were waited for; matrix products, arithmetic and copies ran while one was open for 23% of the time, Pallas kernels for 0%

commit v1 on v0

--- a/solution.py
+++ b/solution.py
@@ -94,7 +94,12 @@
         lax.all_to_all(sent_grads, "expert", split_axis=0, concat_axis=0, tiled=True)
     )
     slot_rows = arrived.shape[0]
-    all_rows = lax.all_gather(arrived, "dp", axis=0, tiled=True)
+    ring = [arrived]
+    for hop in range(15):
+        ring.append(lax.ppermute(ring[-1], "dp", [(dev, (dev + 1) % 16) for dev in range(16)]))
+    all_rows = jnp.roll(
+        jnp.concatenate(ring[::-1], axis=0), (lax.axis_index("dp") + 1) * ring[0].shape[0], axis=0
+    )
     pre = project_up(all_rows, expand_weight)
     hidden = gelu_value(pre).astype(jnp.bfloat16)
     results = lax.psum_scatter(

time: 436 us -> 760 us (1.74)
  waiting for transfers between devices: 219 us -> 470 us
  other arithmetic: 33.5 us -> 85.4 us
  local copies, waits for them, and re-layouts: 45.8 us -> 86.4 us
  blocking collectives: 31.8 us -> 0 us
  starting transfers between devices: 11.1 us -> 25.1 us
    ppermute x0 -> x15, waiting for transfers between devices: none -> 277 us  [body(): lax.ppermute(ring[-1], 'dp', [(dev, (dev + 1) % 16) for dev in range(16)])]
    reduce_scatter x1, waiting for transfers between devices: 0.01 us -> 92.9 us  [body(): lax.psum_scatter(project_down(hidden, reduce_weight).astype(jnp.bfloat16)...]
    all_gather x1, waiting for transfers between devices: 73.6 us -> 0.02 us  [body(): all_grads = lax.all_gather(arrived_grads, 'dp', axis=0, tiled=True)]
    all_gather x1 -> x0, waiting for transfers between devices: 61.1 us -> none  [body(): all_rows = lax.all_gather(arrived, 'dp', axis=0, tiled=True)]
    unnamed x23 -> x96, local copies, waits for them, and re-layouts: 4.25 us -> 52.3 us
    add x16, other arithmetic: 17.2 us -> 64.3 us  [add_block(): return (totals[0] + first_piece, totals[1] + second_piece)]
    all_to_all x2 -> x0, blocking collectives: 31.8 us -> none  [the longest x1 17.6 us: body(): lax.all_to_all(sent_rows, 'expert', split_axis=0, concat_axis=0, tiled=True)]
    while x64 -> x0, local copies, waits for them, and re-layouts: 19 us -> none
  transfers between devices with their start and end apart: 6 -> 22, of which waited for: 4 -> 19; matrix products, arithmetic and copies ran while one was open for 23% -> 28% of each run, Pallas kernels for 0% -> 0%
where the time goes in v1:
time: 760 us; the launch traced here: 758 us
  waiting for transfers between devices  470 us (62%)
  local copies, waits for them, and re-layouts  86.4 us (11%)
  other arithmetic  85.4 us (11%)
  matrix products  76.6 us (10%)
  starting transfers between devices  25.1 us (3%)
  between operations  14.1 us (2%)
    ppermute x15, waiting for transfers between devices, body(): lax.ppermute(ring[-1], 'dp', [(dev, (dev + 1) % 16) for dev in range(16)])  277 us
    reduce_scatter x1, waiting for transfers between devices, body(): lax.psum_scatter(project_down(hidden, reduce_weight).astype(jnp.bfloat16)...  92.9 us
    reduce_scatter x1, waiting for transfers between devices, body(): lax.psum_scatter(project_down(dpre, expand_weight).astype(jnp.bfloat16),...  84.2 us
    add x16, other arithmetic, add_block(): return (totals[0] + first_piece, totals[1] + second_piece)  64.3 us
    unnamed x96, local copies, waits for them, and re-layouts  52.3 us
    dot_general x32, matrix products, outer_rows(): jnp.einsum('rlh,rld->lhd', left, right, preferred_element_type=jnp.float32)  47.9 us
    dot_general x2, matrix products, project_up(): jnp.einsum('rld,lhd->rlh', rows, weight, preferred_element_type=jnp.float32)  17.5 us
  transfers between devices with their start and end apart: 22, of which 19 were waited for; matrix products, arithmetic and copies ran while one was open for 28% of the time, Pallas kernels for 0%

profile of v1, /device:TPU:1, one launch (start us, length us, event | category | flops | bytes accessed | tf_op | source)
XLA Modules:
  0.0 758.1 jit_solution(3646927416570607789)
XLA Ops:
  21.3 6.8 all-to-all-start
  32.7 6.3 all-to-all-done
  45.3 9.7 %all-to-all-done.2 = bf16[8,32,1280]{2,1,0:T(8,128)(2,1)} async-done(((bf16[8,32,1280]{2,1,0:T(8,128)(2,1)}), bf16[8,32,1280]{2,1,0:T(8,128)(2,1)}, u32[]{:S(2)}, u32[]{:S(2)}) %all-to-all-start.2) | async-done | bytes 655392 | tf_op jit(solution)/shard_map/all_to_all | solution.py:94
  57.0 6.9 collective-permute-done
  63.9 28.0 %collective-permute-done.1 = bf16[128,2,1280]{2,0,1:T(8,128)(2,1)S(1)} collective-permute-done((bf16[128,2,1280]{2,0,1:T(8,128)(2,1)S(1)}, bf16[128,2,1280]{2,0,1:T(8,128)(2,1)S(1)}, u32[]{:S(2)}, u32[]{:S(2)}) %collective-permute-start.1) | collective-permute-done | bytes 655392 | tf_op jit(solution)/shard_map/ppermute | solution.py:99
  91.9 21.0 %collective-permute-done.2 = bf16[128,2,1280]{2,0,1:T(8,128)(2,1)S(1)} collective-permute-done((bf16[128,2,1280]{2,0,1:T(8,128)(2,1)S(1)}, bf16[128,2,1280]{2,0,1:T(8,128)(2,1)S(1)}, u32[]{:S(2)}, u32[]{:S(2)}) %collective-permute-start.2) | collective-permute-done | bytes 655392 | tf_op jit(solution)/shard_map/ppermute | solution.py:99
  113.8 31.5 %collective-permute-done.3 = bf16[128,2,1280]{2,0,1:T(8,128)(2,1)S(1)} collective-permute-done((bf16[128,2,1280]{2,0,1:T(8,128)(2,1)S(1)}, bf16[128,2,1280]{2,0,1:T(8,128)(2,1)S(1)}, u32[]{:S(2)}, u32[]{:S(2)}) %collective-permute-start.3) | collective-permute-done | bytes 655392 | tf_op jit(solution)/shard_map/ppermute | solution.py:99
  146.2 31.5 %collective-permute-done.4 = bf16[128,2,1280]{2,0,1:T(8,128)(2,1)S(1)} collective-permute-done((bf16[128,2,1280]{2,0,1:T(8,128)(2,1)S(1)}, bf16[128,2,1280]{2,0,1:T(8,128)(2,1)S(1)}, u32[]{:S(2)}, u32[]{:S(2)}) %collective-permute-start.4) | collective-permute-done | bytes 655392 | tf_op jit(solution)/shard_map/ppermute | solution.py:99
  178.5 14.6 %collective-permute-done.5 = bf16[128,2,1280]{2,0,1:T(8,128)(2,1)S(1)} collective-permute-done((bf16[128,2,1280]{2,0,1:T(8,128)(2,1)S(1)}, bf16[128,2,1280]{2,0,1:T(8,128)(2,1)S(1)}, u32[]{:S(2)}, u32[]{:S(2)}) %collective-permute-start.5) | collective-permute-done | bytes 655392 | tf_op jit(solution)/shard_map/ppermute | solution.py:99
  194.0 13.7 %collective-permute-done.6 = bf16[128,2,1280]{2,0,1:T(8,128)(2,1)S(1)} collective-permute-done((bf16[128,2,1280]{2,0,1:T(8,128)(2,1)S(1)}, bf16[128,2,1280]{2,0,1:T(8,128)(2,1)S(1)}, u32[]{:S(2)}, u32[]{:S(2)}) %collective-permute-start.6) | collective-permute-done | bytes 655392 | tf_op jit(solution)/shard_map/ppermute | solution.py:99
  208.5 12.8 %collective-permute-done.7 = bf16[128,2,1280]{2,0,1:T(8,128)(2,1)S(1)} collective-permute-done((bf16[128,2,1280]{2,0,1:T(8,128)(2,1)S(1)}, bf16[128,2,1280]{2,0,1:T(8,128)(2,1)S(1)}, u32[]{:S(2)}, u32[]{:S(2)}) %collective-permute-start.7) | collective-permute-done | bytes 655392 | tf_op jit(solution)/shard_map/ppermute | solution.py:99
  222.1 13.4 %collective-permute-done.8 = bf16[128,2,1280]{2,0,1:T(8,128)(2,1)S(1)} collective-permute-done((bf16[128,2,1280]{2,0,1:T(8,128)(2,1)S(1)}, bf16[128,2,1280]{2,0,1:T(8,128)(2,1)S(1)}, u32[]{:S(2)}, u32[]{:S(2)}) %collective-permute-start.8) | collective-permute-done | bytes 655392 | tf_op jit(solution)/shard_map/ppermute | solution.py:99
  236.4 14.5 %collective-permute-done.9 = bf16[128,2,1280]{2,0,1:T(8,128)(2,1)S(1)} collective-permute-done((bf16[128,2,1280]{2,0,1:T(8,128)(2,1)S(1)}, bf16[128,2,1280]{2,0,1:T(8,128)(2,1)S(1)}, u32[]{:S(2)}, u32[]{:S(2)}) %collective-permute-start.9) | collective-permute-done | bytes 655392 | tf_op jit(solution)/shard_map/ppermute | solution.py:99
  251.7 15.6 %collective-permute-done.10 = bf16[128,2,1280]{2,0,1:T(8,128)(2,1)S(1)} collective-permute-done((bf16[128,2,1280]{2,0,1:T(8,128)(2,1)S(1)}, bf16[128,2,1280]{2,0,1:T(8,128)(2,1)S(1)}, u32[]{:S(2)}, u32[]{:S(2)}) %collective-permute-start.10) | collective-permute-done | bytes 655392 | tf_op jit(solution)/shard_map/ppermute | solution.py:99
  268.1 19.8 %collective-permute-done.11 = bf16[128,2,1280]{2,0,1:T(8,128)(2,1)S(1)} collective-permute-done((bf16[128,2,1280]{2,0,1:T(8,128)(2,1)S(1)}, bf16[128,2,1280]{2,0,1:T(8,128)(2,1)S(1)}, u32[]{:S(2)}, u32[]{:S(2)}) %collective-permute-start.11) | collective-permute-done | bytes 655392 | tf_op jit(solution)/shard_map/ppermute | solution.py:99
  288.8 19.0 %collective-permute-done.12 = bf16[128,2,1280]{2,0,1:T(8,128)(2,1)S(1)} collective-permute-done((bf16[128,2,1280]{2,0,1:T(8,128)(2,1)S(1)}, bf16[128,2,1280]{2,0,1:T(8,128)(2,1)S(1)}, u32[]{:S(2)}, u32[]{:S(2)}) %collective-permute-start.12) | collective-permute-done | bytes 655392 | tf_op jit(solution)/shard_map/ppermute | solution.py:99
  308.6 18.0 %collective-permute-done.13 = bf16[128,2,1280]{2,0,1:T(8,128)(2,1)} collective-permute-done((bf16[128,2,1280]{2,0,1:T(8,128)(2,1)S(1)}, bf16[128,2,1280]{2,0,1:T(8,128)(2,1)}, u32[]{:S(2)}, u32[]{:S(2)}) %collective-permute-start.13) | collective-permute-done | bytes 655392 | tf_op jit(solution)/shard_map/ppermute | solution.py:99
  326.7 16.8 %collective-permute-done.14 = bf16[128,2,1280]{2,0,1:T(8,128)(2,1)} collective-permute-done((bf16[128,2,1280]{2,0,1:T(8,128)(2,1)}, bf16[128,2,1280]{2,0,1:T(8,128)(2,1)}, u32[]{:S(2)}, u32[]{:S(2)}) %collective-permute-start.14) | collective-permute-done | bytes 655392 | tf_op jit(solution)/shard_map/ppermute | solution.py:99
  383.5 8.5 %constant_dynamic-slice_fusion = bf16[2048,2,1280]{2,0,1:T(8,128)(2,1)} fusion(bf16[4096,2,1280]{2,0,1:T(8,128)(2,1)} %constant_dynamic-update-slice_fusion, s32[]{:T(128)S(6)} %select_n.59), kind=kLoop, calls=%fused_computation.118 | loop fusion | bytes 20971524 | tf_op jit(solution)/shard_map/jit(_roll_dynamic)/dynamic_slice | solution.py:100
  392.0 9.1 %multiply_convert_fusion = (bf16[2048,2,160]{0,2,1:T(8,128)(2,1)S(1)}, f32[2048,2,160]{0,2,1:T(8,128)}) fusion(bf16[2048,2,1280]{2,0,1:T(8,128)(2,1)} %constant_dynamic-slice_fusion, bf16[2,160,1280]{2,1,0:T(8,128)(2,1)S(1)} %copy-done), kind=kOutput, calls=%fused_computation.30 | convolution fusion | flops 1680998400 | bytes 15237120 | tf_op jit(solution)/shard_map/rld,lhd->rlh/dot_general | solution.py:23
  407.9 8.4 %fusion.9 = bf16[2048,2,160]{0,2,1:T(8,128)(2,1)S(1)} fusion(bf16[2048,2,1280]{2,0,1:T(8,128)(2,1)} %all-gather.2.cloned.1.call-done, bf16[2,160,1280]{2,1,0:T(8,128)(2,1)S(1)} %copy-done.29, f32[2048,2,160]{0,2,1:T(8,128)} %get-tuple-element.189), kind=kOutput, calls=%fused_computation.25 | convolution fusion | flops 1684275200 | bytes 15237120 | tf_op jit(solution)/shard_map/rld,lhd->rlh/dot_general | solution.py:23
  423.0 92.9 %reduce-scatter.3.cloned.1.call-done = bf16[128,2,1280]{2,0,1:T(8,128)(2,1)} async-done(((bf16[2048,2,1280]{2,0,1:T(8,128)(2,1)}), bf16[128,2,1280]{2,0,1:T(8,128)(2,1)}) %reduce-scatter.3.cloned.1.call-update) | async-done | bytes 655376 | tf_op jit(solution)/shard_map/reduce_scatter | solution.py:105
  524.0 84.2 %reduce-scatter.5.cloned.1.call-done = bf16[128,2,1280]{2,0,1:T(8,128)(2,1)} async-done(((bf16[2048,2,1280]{2,0,1:T(8,128)(2,1)}), bf16[128,2,1280]{2,0,1:T(8,128)(2,1)}) %reduce-scatter.5.cloned.1.call-update) | async-done | bytes 655376 | tf_op jit(solution)/shard_map/reduce_scatter | solution.py:114
  616.2 112.5 %while.16 = (s32[]{:T(128)}, f32[2,160,1280]{2,1,0:T(8,128)}, f32[2,160,1280]{2,1,0:T(8,128)}, bf16[2048,2,160]{0,2,1:T(8,128)(2,1)}, bf16[2048,2,1280]{2,0,1:T(...) while((s32[]{:T(128)}, f32[2,160,1280]{2,1,0:T(8,128)}, ...), condition=%wide.region_17.18_spmd.clone, body=%wide.region_16.17_spmd.clone.sunk | while | flops 212992000 | bytes 11307173 | solution.py:136
  (237 shorter events, 240.8 us)
Async XLA Ops:
  7.2 384.9 %copy-start = (bf16[2,160,1280]{2,1,0:T(8,128)(2,1)S(1)}, bf16[2,160,1280]{2,1,0:T(8,128)(2,1)}, u32[]{:S(2)}) copy-start(bf16[2,160,1280]{2,1,0:T(8,128)(2,1)} %param.16) | copy-start | bytes 2457604
  21.3 17.7 %all-to-all-start = ((bf16[8,32,1280]{2,1,0:T(8,128)(2,1)}), bf16[8,32,1280]{2,1,0:T(8,128)(2,1)S(1)}, u32[]{:S(2)}, u32[]{:S(2)}) async-start(bf16[8,32,1280]{2,1,0:T(8,128)(2,1)} %broadcast_select_fusion), calls=%async_computation | async-start | bytes 1310720 | tf_op jit(solution)/shard_map/all_to_all | solution.py:92
  39.0 16.0 %all-to-all-start.2 = ((bf16[8,32,1280]{2,1,0:T(8,128)(2,1)}), bf16[8,32,1280]{2,1,0:T(8,128)(2,1)}, u32[]{:S(2)}, u32[]{:S(2)}) async-start(bf16[8,32,1280]{2,1,0:T(8,128)(2,1)} %multiply_convert_fusion.1), calls=%async_computation.3 | async-start | bytes 1310720 | tf_op jit(solution)/shard_map/all_to_all | solution.py:94
  44.0 363.9 %all-gather.2.cloned.1.call-start = ((), (), s32[]{:S(2)}) async-start(), calls=%async_computation.7 | async-start | bytes 11141120 | tf_op jit(solution)/shard_map/all_gather | solution.py:111
  44.0 19.9 %collective-permute-start = (bf16[128,2,1280]{2,0,1:T(8,128)(2,1)S(1)}, bf16[128,2,1280]{2,0,1:T(8,128)(2,1)S(1)}, u32[]{:S(2)}, u32[]{:S(2)}) collective-permute-start(bf16[128,2,1280]{2,0,1:T(8,128)(2,1)S(1)} %bitcast.64), channel_id=1, source_target_pairs={{0,8},{8,16},{16,24},{24,32},{32,40},{40,48},{48,56},{56,64},{64,7... | collective-permute-start | bytes 1966088 | tf_op jit(solution)/shard_map/ppermute | solution.py:99
  57.0 459.0 %reduce-scatter.3.cloned.1.call-start = ((), (), s32[]{:S(2)}) async-start(), calls=%async_computation.6 | async-start | bytes 11141120 | tf_op jit(solution)/shard_map/reduce_scatter | solution.py:105
  63.9 28.0 %collective-permute-start.1 = (bf16[128,2,1280]{2,0,1:T(8,128)(2,1)S(1)}, bf16[128,2,1280]{2,0,1:T(8,128)(2,1)S(1)}, u32[]{:S(2)}, u32[]{:S(2)}) collective-permute-start(bf16[128,2,1280]{2,0,1:T(8,128)(2,1)S(1)} %collective-permute-done), channel_id=1, source_target_pairs={{0,8},{8,16},{16,24},{24,32},{32,40},{40,48},{48,56},{56,64},{64,7... | collective-permute-start | bytes 1966088 | tf_op jit(solution)/shard_map/ppermute | solution.py:99
  91.9 21.0 %collective-permute-start.2 = (bf16[128,2,1280]{2,0,1:T(8,128)(2,1)S(1)}, bf16[128,2,1280]{2,0,1:T(8,128)(2,1)S(1)}, u32[]{:S(2)}, u32[]{:S(2)}) collective-permute-start(bf16[128,2,1280]{2,0,1:T(8,128)(2,1)S(1)} %collective-permute-done.1), channel_id=1, source_target_pairs={{0,8},{8,16},{16,24},{24,32},{32,40},{40,48},{48,56},{56,64},{64,7... | collective-permute-start | bytes 1966088 | tf_op jit(solution)/shard_map/ppermute | solution.py:99
  113.8 31.5 %collective-permute-start.3 = (bf16[128,2,1280]{2,0,1:T(8,128)(2,1)S(1)}, bf16[128,2,1280]{2,0,1:T(8,128)(2,1)S(1)}, u32[]{:S(2)}, u32[]{:S(2)}) collective-permute-start(bf16[128,2,1280]{2,0,1:T(8,128)(2,1)S(1)} %collective-permute-done.2), channel_id=1, source_target_pairs={{0,8},{8,16},{16,24},{24,32},{32,40},{40,48},{48,56},{56,64},{64,7... | collective-permute-start | bytes 1966088 | tf_op jit(solution)/shard_map/ppermute | solution.py:99
  146.1 31.5 %collective-permute-start.4 = (bf16[128,2,1280]{2,0,1:T(8,128)(2,1)S(1)}, bf16[128,2,1280]{2,0,1:T(8,128)(2,1)S(1)}, u32[]{:S(2)}, u32[]{:S(2)}) collective-permute-start(bf16[128,2,1280]{2,0,1:T(8,128)(2,1)S(1)} %collective-permute-done.3), channel_id=1, source_target_pairs={{0,8},{8,16},{16,24},{24,32},{32,40},{40,48},{48,56},{56,64},{64,7... | collective-permute-start | bytes 1966088 | tf_op jit(solution)/shard_map/ppermute | solution.py:99
  178.5 14.6 %collective-permute-start.5 = (bf16[128,2,1280]{2,0,1:T(8,128)(2,1)S(1)}, bf16[128,2,1280]{2,0,1:T(8,128)(2,1)S(1)}, u32[]{:S(2)}, u32[]{:S(2)}) collective-permute-start(bf16[128,2,1280]{2,0,1:T(8,128)(2,1)S(1)} %collective-permute-done.4), channel_id=1, source_target_pairs={{0,8},{8,16},{16,24},{24,32},{32,40},{40,48},{48,56},{56,64},{64,7... | collective-permute-start | bytes 1966088 | tf_op jit(solution)/shard_map/ppermute | solution.py:99
  194.0 13.7 %collective-permute-start.6 = (bf16[128,2,1280]{2,0,1:T(8,128)(2,1)S(1)}, bf16[128,2,1280]{2,0,1:T(8,128)(2,1)S(1)}, u32[]{:S(2)}, u32[]{:S(2)}) collective-permute-start(bf16[128,2,1280]{2,0,1:T(8,128)(2,1)S(1)} %collective-permute-done.5), channel_id=1, source_target_pairs={{0,8},{8,16},{16,24},{24,32},{32,40},{40,48},{48,56},{56,64},{64,7... | collective-permute-start | bytes 1966088 | tf_op jit(solution)/shard_map/ppermute | solution.py:99
  208.5 12.8 %collective-permute-start.7 = (bf16[128,2,1280]{2,0,1:T(8,128)(2,1)S(1)}, bf16[128,2,1280]{2,0,1:T(8,128)(2,1)S(1)}, u32[]{:S(2)}, u32[]{:S(2)}) collective-permute-start(bf16[128,2,1280]{2,0,1:T(8,128)(2,1)S(1)} %collective-permute-done.6), channel_id=1, source_target_pairs={{0,8},{8,16},{16,24},{24,32},{32,40},{40,48},{48,56},{56,64},{64,7... | collective-permute-start | bytes 1966088 | tf_op jit(solution)/shard_map/ppermute | solution.py:99
  222.1 13.4 %collective-permute-start.8 = (bf16[128,2,1280]{2,0,1:T(8,128)(2,1)S(1)}, bf16[128,2,1280]{2,0,1:T(8,128)(2,1)S(1)}, u32[]{:S(2)}, u32[]{:S(2)}) collective-permute-start(bf16[128,2,1280]{2,0,1:T(8,128)(2,1)S(1)} %collective-permute-done.7), channel_id=1, source_target_pairs={{0,8},{8,16},{16,24},{24,32},{32,40},{40,48},{48,56},{56,64},{64,7... | collective-permute-start | bytes 1966088 | tf_op jit(solution)/shard_map/ppermute | solution.py:99
  236.4 14.5 %collective-permute-start.9 = (bf16[128,2,1280]{2,0,1:T(8,128)(2,1)S(1)}, bf16[128,2,1280]{2,0,1:T(8,128)(2,1)S(1)}, u32[]{:S(2)}, u32[]{:S(2)}) collective-permute-start(bf16[128,2,1280]{2,0,1:T(8,128)(2,1)S(1)} %collective-permute-done.8), channel_id=1, source_target_pairs={{0,8},{8,16},{16,24},{24,32},{32,40},{40,48},{48,56},{56,64},{64,7... | collective-permute-start | bytes 1966088 | tf_op jit(solution)/shard_map/ppermute | solution.py:99
  251.7 15.6 %collective-permute-start.10 = (bf16[128,2,1280]{2,0,1:T(8,128)(2,1)S(1)}, bf16[128,2,1280]{2,0,1:T(8,128)(2,1)S(1)}, u32[]{:S(2)}, u32[]{:S(2)}) collective-permute-start(bf16[128,2,1280]{2,0,1:T(8,128)(2,1)S(1)} %collective-permute-done.9), channel_id=1, source_target_pairs={{0,8},{8,16},{16,24},{24,32},{32,40},{40,48},{48,56},{56,64},{64,7... | collective-permute-start | bytes 1966088 | tf_op jit(solution)/shard_map/ppermute | solution.py:99
  268.1 19.8 %collective-permute-start.11 = (bf16[128,2,1280]{2,0,1:T(8,128)(2,1)S(1)}, bf16[128,2,1280]{2,0,1:T(8,128)(2,1)S(1)}, u32[]{:S(2)}, u32[]{:S(2)}) collective-permute-start(bf16[128,2,1280]{2,0,1:T(8,128)(2,1)S(1)} %collective-permute-done.10), channel_id=1, source_target_pairs={{0,8},{8,16},{16,24},{24,32},{32,40},{40,48},{48,56},{56,64},{64,7... | collective-permute-start | bytes 1966088 | tf_op jit(solution)/shard_map/ppermute | solution.py:99
  288.8 19.0 %collective-permute-start.12 = (bf16[128,2,1280]{2,0,1:T(8,128)(2,1)S(1)}, bf16[128,2,1280]{2,0,1:T(8,128)(2,1)S(1)}, u32[]{:S(2)}, u32[]{:S(2)}) collective-permute-start(bf16[128,2,1280]{2,0,1:T(8,128)(2,1)S(1)} %collective-permute-done.11), channel_id=1, source_target_pairs={{0,8},{8,16},{16,24},{24,32},{32,40},{40,48},{48,56},{56,64},{64,7... | collective-permute-start | bytes 1966088 | tf_op jit(solution)/shard_map/ppermute | solution.py:99
  308.6 18.0 %collective-permute-start.13 = (bf16[128,2,1280]{2,0,1:T(8,128)(2,1)S(1)}, bf16[128,2,1280]{2,0,1:T(8,128)(2,1)}, u32[]{:S(2)}, u32[]{:S(2)}) collective-permute-start(bf16[128,2,1280]{2,0,1:T(8,128)(2,1)S(1)} %collective-permute-done.12), channel_id=1, source_target_pairs={{0,8},{8,16},{16,24},{24,32},{32,40},{40,48},{48,56},{56,64},{64,7... | collective-permute-start | bytes 1966088 | tf_op jit(solution)/shard_map/ppermute | solution.py:99
  326.6 16.8 %collective-permute-start.14 = (bf16[128,2,1280]{2,0,1:T(8,128)(2,1)}, bf16[128,2,1280]{2,0,1:T(8,128)(2,1)}, u32[]{:S(2)}, u32[]{:S(2)}) collective-permute-start(bf16[128,2,1280]{2,0,1:T(8,128)(2,1)} %collective-permute-done.13), channel_id=1, source_target_pairs={{0,8},{8,16},{16,24},{24,32},{32,40},{40,48},{48,56},{56,64},{64,7... | collective-permute-start | bytes 1966088 | tf_op jit(solution)/shard_map/ppermute | solution.py:99
  326.6 36.7 %copy-start.5 = (bf16[128,2,1280]{2,0,1:T(8,128)(2,1)S(1)}, bf16[128,2,1280]{2,0,1:T(8,128)(2,1)}, u32[]{:S(2)}) copy-start(bf16[128,2,1280]{2,0,1:T(8,128)(2,1)} %copy-done.4) | copy-start | bytes 1966084
  407.8 200.4 %reduce-scatter.5.cloned.1.call-start = ((), (), s32[]{:S(2)}) async-start(), calls=%async_computation.8 | async-start | bytes 11141120 | tf_op jit(solution)/shard_map/reduce_scatter | solution.py:114
  517.9 92.3 %all-to-all-start.1 = ((bf16[8,32,1280]{2,1,0:T(8,128)(2,1)}), bf16[8,32,1280]{2,1,0:T(8,128)(2,1)S(1)}, u32[]{:S(2)}, u32[]{:S(2)}) async-start(bf16[8,32,1280]{2,1,0:T(8,128)(2,1)} %bitcast.13), calls=%async_computation.2 | async-start | bytes 1310720 | tf_op jit(solution)/shard_map/all_to_all | solution.py:141
  610.2 133.0 %all-to-all-start.3 = ((bf16[8,32,1280]{2,1,0:T(8,128)(2,1)}), bf16[8,32,1280]{2,1,0:T(8,128)(2,1)}, u32[]{:S(2)}, u32[]{:S(2)}) async-start(bf16[8,32,1280]{2,1,0:T(8,128)(2,1)} %bitcast.23), calls=%async_computation.5 | async-start | bytes 1310720 | tf_op jit(solution)/shard_map/all_to_all | solution.py:151
  (29 other events, 364.6 us)
Sparse Core Ops, SparseCore 0:
  57.1 121.5 all-gather.1
  407.9 107.9 reduce-scatter.2
  519.4 88.7 reduce-scatter.4
